TPU v7x, 32 devices: a whole 2x2x4 slice. The times are simulated.
32 devices in a mesh: chan: 8 (over z, x), tile: 4 (over y, core).
Axes of the slice: x: 2, y: 2, z: 4, core: 2. Of those that a mesh axis runs over, the one named last changes fastest.
Arguments:
- voltages: bfloat16 [2, 1024, 5888], P(None, 'chan'), may hold values from -6 to 6
- taps: float32 [16, 256], replicated, may hold values from -0.09375 to 0.09375
- beam_weights: bfloat16 [2, 256, 64, 1024], P(None, 'chan'), may hold values from -0.1875 to 0.1875
- station_masks: int32 [64, 512], replicated, may hold values 0 or 1
- tile_pairs: int32 [36, 2], P('tile'), may hold values from 0 to 7, as said below
Outputs:
- visibilities: float32 [2, 256, 36, 128, 128], P(None, 'chan', 'tile')
- beams: bfloat16 [2, 64, 8, 256], P(None, 'tile', 'chan')
Inputs may be any that keep to these rules, and one draw needn't show every extreme that they name: `tile_pairs`: each pair (r, s) with 0 <= s <= r < 8 stands in exactly one row, r in the first column and s in the second.
All inputs are finite; a program needn't handle non-finite values.
Results may differ from a plain program's by a relative error of at most 0.0049.
Values may be sent and summed in bfloat16 or wider, within the bound.
A program may use at most 128 MiB of HBM per device.

v0:
```python
import math

import jax
import jax.numpy as jnp
from jax import lax
from jax.sharding import PartitionSpec as P

TB = 128


def dft_table(channels):
    counter = jnp.arange(channels, dtype=jnp.int32)
    wrapped = counter[:, None] * counter[None, :] % channels
    phases = 2.0 * math.pi / channels * wrapped.astype(jnp.float32)
    cosine = jnp.cos(phases)
    sine_part = jnp.sin(phases)
    first_row = jnp.stack([cosine, sine_part], axis=1)
    second_row = jnp.stack([-sine_part, cosine], axis=1)
    return jnp.stack([first_row, second_row], axis=1)


def filterbank(voltages, taps, count):
    taps_count, channels = taps.shape
    in_dev = voltages.shape[1]
    framed = voltages.reshape(2, in_dev, count + taps_count - 1, channels)
    frames = jnp.zeros((2, in_dev, count, channels), jnp.float32)
    for tap_index in range(taps_count):
        frames = frames + taps[tap_index] * framed[:, :, tap_index : tap_index + count, :].astype(
            jnp.float32
        )
    spectra = jnp.einsum(
        "crsk,sitk->crit",
        dft_table(channels),
        frames,
        precision=lax.Precision.HIGHEST,
        preferred_element_type=jnp.float32,
    )
    return spectra.astype(jnp.bfloat16)


def correlate(time_piece, tile_pairs):
    chan_dev = time_piece.shape[0]
    inputs = time_piece.shape[2]
    time_width = time_piece.shape[3]
    blocks = time_piece.reshape(chan_dev, 2, inputs // TB, TB, time_width)
    left_rows = jnp.take(blocks, tile_pairs[:, 0], axis=2)
    right_rows = jnp.take(blocks, tile_pairs[:, 1], axis=2)
    rotated = jnp.stack([left_rows[:, 1], -left_rows[:, 0]], axis=1)
    stacked = jnp.stack([left_rows, rotated], axis=0)
    return jnp.einsum(
        "ocrkaw,crkbw->ockab", stacked, right_rows, preferred_element_type=jnp.float32
    )


def beamform(own_time, beam_weights, station_masks):
    beams_count, stations = station_masks.shape
    live_inputs = jnp.broadcast_to(station_masks[:, :, None], (beams_count, stations, 2))
    live_inputs = live_inputs.reshape(beams_count, 2 * stations).astype(jnp.bfloat16)
    weights = beam_weights * live_inputs[None, None]
    products = jnp.einsum("scbi,crit->csrbt", weights, own_time, preferred_element_type=jnp.float32)
    real_part = products[:, 0, 0] - products[:, 1, 1]
    imag_part = products[:, 0, 1] + products[:, 1, 0]
    return jnp.transpose(jnp.stack([real_part, imag_part]), (0, 2, 3, 1)).astype(jnp.bfloat16)


def on_device(voltages, taps, beam_weights, station_masks, tile_pairs):
    taps_count, channels = taps.shape
    tile_count = lax.axis_size("tile")
    total_time = voltages.shape[2] // channels - taps_count + 1
    quarter = total_time // tile_count
    tile_index = lax.axis_index("tile")
    spectra = filterbank(voltages, taps, total_time)
    turned = lax.all_to_all(spectra, "chan", split_axis=0, concat_axis=2, tiled=True)
    own_time = lax.dynamic_slice_in_dim(turned, tile_index * quarter, quarter, 3)
    visibility = correlate(turned, tile_pairs)
    visibility = visibility * (1.0 / total_time)
    beam_part = beamform(own_time, beam_weights, station_masks)
    beams = lax.all_to_all(
        lax.all_to_all(beam_part, "tile", split_axis=1, concat_axis=2, tiled=True),
        "chan",
        split_axis=2,
        concat_axis=3,
        tiled=True,
    )
    return (visibility, beams)


def solution(mesh):
    in_specs = (P(None, "chan", None), P(), P(None, "chan", None, None), P(), P("tile", None))
    out_specs = (P(None, "chan", "tile", None, None), P(None, "tile", "chan", None))
    return jax.shard_map(
        on_device, mesh=mesh, in_specs=in_specs, out_specs=out_specs, check_vma=False
    )
```

profile of v0, /device:TPU:0, one launch (start us, length us, event | category | flops | bytes accessed | tf_op | source)
XLA Modules:
  0.0 124.9 jit_solution(12216933234083120169)
XLA Ops:
  0.6 1.0 fusion.109
  1.6 1.7 %fusion.107 = (f32[256,1,256]{2,0,1:T(8,128)S(1)}, f32[256,1,256]{2,0,1:T(8,128)}) fusion(), kind=kLoop, calls=%fused_computation.119 | loop fusion | flops 917504 | bytes 524288 | tf_op jit(solution)/shard_map/sin | solution.py:16
  3.3 1.7 %fusion.119 = (f32[1,256]{1,0:T(1,128)S(1)}, f32[1,256]{1,0:T(1,128)S(1)}, f32[1,256]{1,0:T(1,128)S(1)}, f32[1,256]{1,0:T(1,128)S(1)}, f32[1,256]{1,0:T(1,128)},...) fusion(f32[16,256]{1,0:T(8,128)} %param.8), kind=kLoop, calls=%fused_computation.141 | loop fusion | bytes 32768 | tf_op jit(solution)/shard_map/slice | solution.py:28
  5.0 3.5 %copy.96 = bf16[2,128,5888]{1,2,0:T(8,128)(2,1)S(1)} copy(bf16[2,128,5888]{2,1,0:T(8,128)(2,1)} %param.7) | data formatting | bytes 6029312 | tf_op args[0]
  8.5 1.1 maximum_bitcast_fusion.1
  9.6 7.1 %bitcast_convert_fusion = bf16[256,2,128,8]{2,0,3,1:T(8,128)(2,1)S(1)} fusion(bf16[2,128,23,256]{1,3,2,0:T(8,128)(2,1)S(1)} %bitcast.122, f32[256,1,2,256]{3,0,2,1:T(8,128)S(1)} %get-tuple-element.26, f32[256,1,2,256]{3,0,2,1:T(8,128)S(1)} %get-tuple-element.25, f32[256]{0:T(256)} %bitcast.145, f32[256]{0:T(256)} %bitcast.146, f32[256]{0:T(256)S(1)} %bitcast.132, ...), kind=kOutput, calls=%fused_computation.10 | convolution fusion | flops 3246653440 | bytes 18890752 | tf_op jit(solution)/shard_map/crsk,sitk->crit/dot_general | solution.py:31
  16.7 1.6 %copy.98 = bf16[256,2,128,8]{2,3,1,0:T(8,128)(2,1)} copy(bf16[256,2,128,8]{2,0,3,1:T(8,128)(2,1)S(1)} %bitcast_convert_fusion) | data formatting | bytes 2097152 | tf_op jit(solution)/shard_map/convert_element_type | solution.py:38
  18.4 7.4 %all-to-all-start = ((bf16[256,2,128,8]{2,3,1,0:T(8,128)(2,1)}), bf16[256,2,128,8]{2,3,1,0:T(8,128)(2,1)S(1)}, u32[]{:S(2)}, u32[]{:S(2)}) async-start(bf16[256,2,128,8]{2,3,1,0:T(8,128)(2,1)} %copy.98), calls=%async_computation | async-start | bytes 2097152 | tf_op jit(solution)/shard_map/all_to_all | solution.py:73
  26.2 25.3 %all-to-all-done = bf16[256,2,128,8]{2,3,1,0:T(8,128)(2,1)S(1)} async-done(((bf16[256,2,128,8]{2,3,1,0:T(8,128)(2,1)}), bf16[256,2,128,8]{2,3,1,0:T(8,128)(2,1)S(1)}, u32[]{:S(2)}, u32[]{:S(2)}) %all-to-all-start) | async-done | bytes 1048608 | tf_op jit(solution)/shard_map/all_to_all | solution.py:73
  51.5 0.3 copy.144
  51.8 6.9 %fusion.58 = f32[32,2,2,64,2]{3,4,1,2,0:T(2,128)S(1)} fusion(bf16[32,2,1024,8]{2,3,1,0:T(8,128)(2,1)S(1)} %bitcast.118, s32[]{:T(128)S(6)} %select_n.39, bf16[2,32,64,1024]{3,2,1,0:T(8,128)(2,1)} %param.9, bf16[64,1024]{1,0:T(8,128)(2,1)S(1)} %copy.104), kind=kOutput, calls=%fused_computation.64 | convolution fusion | flops 37748736 | bytes 8847364 | tf_op jit(solution)/shard_map/scbi,crit->csrbt/dot_general | solution.py:60
  58.9 0.7 reshape.184
  59.7 3.3 %all-to-all-start.1 = ((bf16[4,2,1024]{2,1,0:T(2,128)(2,1)}), bf16[4,2,1024]{2,1,0:T(2,128)(2,1)S(1)}, u32[]{:S(2)}, u32[]{:S(2)}) async-start(bf16[4,2,1024]{2,1,0:T(2,128)(2,1)} %reshape.184), calls=%async_computation.1 | async-start | bytes 32768 | tf_op jit(solution)/shard_map/all_to_all | solution.py:79
  62.9 1.0 gather_fusion.1
  63.9 1.2 fusion.97
  65.1 0.2 fusion.118
  65.3 0.2 maximum_bitcast_fusion
  65.5 1.0 gather_fusion
  66.5 0.2 all-to-all-done.1
  66.9 0.7 reshape.186
  67.6 3.6 %all-to-all-start.2 = ((bf16[8,2,512]{2,1,0:T(2,128)(2,1)}), bf16[8,2,512]{2,1,0:T(2,128)(2,1)S(1)}, u32[]{:S(2)}, u32[]{:S(2)}) async-start(bf16[8,2,512]{2,1,0:T(2,128)(2,1)} %reshape.186), calls=%async_computation.2 | async-start | bytes 32768 | tf_op jit(solution)/shard_map/all_to_all | solution.py:78
  71.2 16.0 %fusion = f32[2,32,9,128,128]{3,4,0,2,1:T(8,128)} fusion(bf16[1,32,2,9,128,8]{4,5,2,0,3,1:T(8,128)(2,1)S(1)} %maximum_bitcast_fusion, bf16[1,32,2,9,128,8]{4,5,2,0,3,1:T(8,128)(2,1)} %get-tuple-element.19, bf16[9,32,2,128,8]{3,4,2,1,0:T(8,128)(2,1)S(1)} %gather_fusion, pred[9]{0:T(512)(128)(4,1)S(1)} %get-tuple-element.15), kind=kOutput, calls=%fused_computation.3 | convolution fusion | flops 316735488 | bytes 41287688 | tf_op jit(solution)/shard_map/ocrkaw,crkbw->ockab/dot_general | solution.py:50
  87.2 36.9 %copy.113 = f32[2,32,9,128,128]{4,3,2,1,0:T(8,128)} copy(f32[2,32,9,128,128]{3,4,0,2,1:T(8,128)} %fusion) | data formatting | bytes 75497472
  124.2 0.7 all_to_all.44
  (21 shorter events, 0.9 us)
Async XLA Ops:
  16.7 9.1 %copy-start = (s32[64,512]{1,0:T(8,128)S(1)}, s32[64,512]{1,0:T(8,128)}, u32[]{:S(2)}) copy-start(s32[64,512]{1,0:T(8,128)} %param.10) | copy-start | bytes 393220
  18.4 7.8 %copy-start.1 = (s32[9,2]{0,1:T(2,128)S(1)}, s32[9,2]{0,1:T(2,128)}, u32[]{:S(2)}) copy-start(s32[9,2]{0,1:T(2,128)} %param.11) | copy-start | bytes 220
  18.4 33.2 %all-to-all-start = ((bf16[256,2,128,8]{2,3,1,0:T(8,128)(2,1)}), bf16[256,2,128,8]{2,3,1,0:T(8,128)(2,1)S(1)}, u32[]{:S(2)}, u32[]{:S(2)}) async-start(bf16[256,2,128,8]{2,3,1,0:T(8,128)(2,1)} %copy.98), calls=%async_computation | async-start | bytes 2097152 | tf_op jit(solution)/shard_map/all_to_all | solution.py:73
  59.7 7.1 %all-to-all-start.1 = ((bf16[4,2,1024]{2,1,0:T(2,128)(2,1)}), bf16[4,2,1024]{2,1,0:T(2,128)(2,1)S(1)}, u32[]{:S(2)}, u32[]{:S(2)}) async-start(bf16[4,2,1024]{2,1,0:T(2,128)(2,1)} %reshape.184), calls=%async_computation.1 | async-start | bytes 32768 | tf_op jit(solution)/shard_map/all_to_all | solution.py:79
  67.6 56.5 %all-to-all-start.2 = ((bf16[8,2,512]{2,1,0:T(2,128)(2,1)}), bf16[8,2,512]{2,1,0:T(2,128)(2,1)S(1)}, u32[]{:S(2)}, u32[]{:S(2)}) async-start(bf16[8,2,512]{2,1,0:T(2,128)(2,1)} %reshape.186), calls=%async_computation.2 | async-start | bytes 32768 | tf_op jit(solution)/shard_map/all_to_all | solution.py:78
where the time goes:
time: 126 us; the launch traced here: 125 us
  local copies, waits for them, and re-layouts  48.9 us (39%)
  matrix products  29.9 us (24%)
  waiting for transfers between devices  25.5 us (20%)
  starting transfers between devices  14.2 us (11%)
  other arithmetic  5.54 us (4%)
    unnamed x10, local copies, waits for them, and re-layouts  42 us
    all_to_all x1, waiting for transfers between devices, on_device(): lax.all_to_all(spectra, 'chan', split_axis=0, concat_axis=2, tiled=True)  25.3 us
    dot_general x1, matrix products, correlate(): jnp.einsum('ocrkaw,crkbw->ockab', stacked, right_rows, preferred_element_...  16 us
    all_to_all x1, starting transfers between devices, on_device(): lax.all_to_all(spectra, 'chan', split_axis=0, concat_axis=2, tiled=True)  7.38 us
    dot_general x1, matrix products, filterbank(): jnp.einsum('crsk,sitk->crit', dft_table(channels), frames, precision=lax....  7.12 us
    dot_general x1, matrix products, beamform(): jnp.einsum('scbi,crit->csrbt', weights, own_time, preferred_element_type=...  6.86 us
    all_to_all x1, starting transfers between devices, on_device(): lax.all_to_all(lax.all_to_all(beam_part, 'tile', split_axis=1, concat_axi...  3.59 us
    all_to_all x1, starting transfers between devices, on_device(): lax.all_to_all(beam_part, 'tile', split_axis=1, concat_axis=2, tiled=True)  3.25 us
  transfers between devices with their start and end apart: 3, of which 2 were waited for; matrix products, arithmetic and copies ran while one was open for 46% of the time, Pallas kernels for 0%

commit v1 on v0

v1 whole, which is shorter than its diff:
```python
import functools
import math

import jax
import jax.numpy as jnp
import numpy as np
from jax import lax
from jax.experimental import pallas as pl
from jax.experimental.pallas import tpu as pltpu
from jax.sharding import PartitionSpec as P

TB = 128
MESH = pl.DeviceIdType.MESH
TURN_KERNEL = False


def dft_table(channels):
    counter = np.arange(channels, dtype=np.int64)
    phases = 2.0 * math.pi / channels * (counter[:, None] * counter[None, :] % channels)
    cosine, sine = np.cos(phases), np.sin(phases)
    first_row = np.stack([cosine, sine], axis=1)
    second_row = np.stack([-sine, cosine], axis=1)
    return np.stack([first_row, second_row], axis=1).astype(np.float32)


def filterbank(voltages, taps, count):
    taps_count, channels = taps.shape
    in_dev = voltages.shape[1]
    framed = voltages.reshape(2, in_dev, count + taps_count - 1, channels)
    frames = jnp.zeros((2, in_dev, count, channels), jnp.float32)
    for p in range(taps_count):
        frames = frames + taps[p] * framed[:, :, p : p + count, :].astype(jnp.float32)
    spectra = jnp.einsum(
        "csrk,ritk->csti",
        jnp.asarray(dft_table(channels)),
        frames,
        precision=lax.Precision.HIGHEST,
        preferred_element_type=jnp.float32,
    )
    return spectra.astype(jnp.bfloat16)


def turn_kernel(n, tq, volts, taps_ref, hi_ref, lo_ref, out, send, s1, r1, s2, r2, s3, r3, s4, r4):
    me = lax.axis_index("chan")
    tile = lax.axis_index("tile")
    far = lax.rem(tile + 2, 4)
    near = tile + 1 - 2 * lax.rem(tile, 2)
    taps_count, channels = taps_ref.shape
    rows = out.shape[2] // tq
    width = out.shape[3]

    barrier = pltpu.get_barrier_semaphore()

    @pl.loop(1, n)
    def _(k):
        pl.semaphore_signal(
            barrier, inc=1, device_id=(lax.rem(me + k, n), tile), device_id_type=MESH
        )

    for t in (far, near):
        pl.semaphore_signal(barrier, inc=1, device_id=(me, t), device_id_type=MESH)

    for t in range(tq):
        parts = []
        for r in range(2):
            total = jnp.zeros((width, channels), jnp.float32)
            for p in range(taps_count):
                at = pl.multiple_of((tile * tq + t + p) * channels, channels)
                total = total + taps_ref[p : p + 1, :] * volts[r, :, pl.ds(at, channels)].astype(
                    jnp.float32
                )
            parts.append(total)
        frame = jnp.concatenate(parts, axis=1)
        high = frame.astype(jnp.bfloat16)
        low = (frame - high.astype(jnp.float32)).astype(jnp.bfloat16)

        def nt(a, b):
            return lax.dot_general(
                a, b, (((1,), (1,)), ((), ())), preferred_element_type=jnp.float32
            )

        got = nt(hi_ref[...], high) + nt(hi_ref[...], low) + nt(lo_ref[...], high)
        send[:, t * rows : (t + 1) * rows, :] = got.astype(jnp.bfloat16).reshape(n, rows, width)

    pl.semaphore_wait(barrier, n + 1)

    def first(k, src):
        d = lax.rem(me + k, n)
        return pltpu.make_async_remote_copy(
            src_ref=send.at[d],
            dst_ref=out.at[src, tile],
            send_sem=s1.at[d],
            recv_sem=r1.at[src],
            device_id=(d, tile),
            device_id_type=MESH,
        )

    def onward(j, block, peer, ss, rr):
        return pltpu.make_async_remote_copy(
            src_ref=out.at[j, block],
            dst_ref=out.at[j, block],
            send_sem=ss.at[j],
            recv_sem=rr.at[j],
            device_id=(me, peer),
            device_id_type=MESH,
        )

    @pl.loop(1, n)
    def _(k):
        first(k, me).start()

    out[me, tile] = send[me]

    @pl.loop(0, n)
    def _(k):
        j = lax.rem(me + n - k, n)

        @pl.when(k > 0)
        def _():
            first(1, j).wait_recv()

        onward(j, tile, far, s2, r2).start()
        onward(j, tile, near, s3, r3).start()

    @pl.loop(0, n)
    def _(k):
        j = lax.rem(me + n - k, n)
        onward(j, far, far, s2, r2).wait_recv()
        onward(j, far, near, s4, r4).start()

    @pl.loop(0, n)
    def _(k):
        j = lax.rem(me + n - k, n)
        other = lax.rem(near + 2, 4)
        onward(j, near, near, s3, r3).wait_recv()
        onward(j, other, near, s4, r4).wait_recv()
        onward(j, tile, far, s2, r2).wait_send()
        onward(j, tile, near, s3, r3).wait_send()
        onward(j, far, near, s4, r4).wait_send()

        @pl.when(k > 0)
        def _():
            first(k, me).wait_send()


def turn(voltages, taps, total_time):
    taps_count, channels = taps.shape
    n = lax.axis_size("chan")
    tiles = lax.axis_size("tile")
    width = voltages.shape[1]
    cd = channels // n
    tq = total_time // tiles
    table = dft_table(channels).reshape(n, cd, 2, 2 * channels)
    table = table.transpose(0, 2, 1, 3).reshape(n * 2 * cd, 2 * channels)
    high = table.astype(jnp.bfloat16)
    low = (table - high.astype(np.float32)).astype(jnp.bfloat16)
    rows = tq * 2 * cd
    sem = [pltpu.SemaphoreType.DMA((n,))] * 8
    got = pl.pallas_call(
        functools.partial(turn_kernel, n, tq),
        out_shape=jax.ShapeDtypeStruct((n, tiles, rows, width), jnp.bfloat16),
        in_specs=[pl.BlockSpec(memory_space=pltpu.VMEM)] * 4,
        out_specs=pl.BlockSpec(memory_space=pltpu.VMEM),
        scratch_shapes=[pltpu.VMEM((n, rows, width), jnp.bfloat16)] + sem,
        compiler_params=pltpu.CompilerParams(
            collective_id=0, has_side_effects=True, vmem_limit_bytes=40 * 2**20
        ),
    )(voltages, taps, jnp.asarray(high), jnp.asarray(low))
    got = got.reshape(n, tiles, tq, 2, cd, width).transpose(4, 3, 1, 2, 0, 5)
    return got.reshape(cd, 2 * total_time, n * width)


def beam_kernel(time, where, w_ref, mask_ref, x_ref, out):
    beams = mask_ref.shape[0]
    mask = mask_ref[...]
    for c in range(x_ref.shape[0]):
        x = x_ref[c]
        prod = []
        for s in range(2):
            w = w_ref[s, c] * mask
            prod.append(
                lax.dot_general(
                    w, x, (((1,), (1,)), ((), ())), preferred_element_type=jnp.float32
                )
            )
        out[c, 0] = prod[0][:, :time] - prod[1][:, time:]
        out[c, 1] = prod[0][:, time:] + prod[1][:, :time]


def beamform(x, beam_weights, station_masks, tile_index):
    cd, rows, inputs = x.shape
    tiles = lax.axis_size("tile")
    beams = station_masks.shape[0] // tiles
    own = lax.dynamic_slice_in_dim(station_masks, tile_index * beams, beams, 0)
    live = jnp.repeat(own, 2, axis=1).astype(jnp.bfloat16)
    step = math.gcd(cd, 8)
    return pl.pallas_call(
        functools.partial(beam_kernel, rows // 2),
        out_shape=jax.ShapeDtypeStruct((cd, 2, beams, rows // 2), jnp.float32),
        grid_spec=pltpu.PrefetchScalarGridSpec(
            num_scalar_prefetch=1,
            grid=(cd // step,),
            in_specs=[
                pl.BlockSpec((2, step, beams, inputs), lambda i, at: (0, i, at[0], 0)),
                pl.BlockSpec((beams, inputs), lambda i, at: (0, 0)),
                pl.BlockSpec((step, rows, inputs), lambda i, at: (i, 0, 0)),
            ],
            out_specs=pl.BlockSpec((step, 2, beams, rows // 2), lambda i, at: (i, 0, 0, 0)),
        ),
        compiler_params=pltpu.CompilerParams(vmem_limit_bytes=40 * 2**20),
    )(tile_index[None].astype(jnp.int32), beam_weights, live, x)


def correlate_kernel(scale, pairs, x_ref, y_ref, out):
    for c in range(x_ref.shape[0]):
        for n in range(out.shape[2]):
            u = pl.ds(pl.multiple_of(pairs[n, 0] * TB, TB), TB)
            v = pl.ds(pl.multiple_of(pairs[n, 1] * TB, TB), TB)
            right = jnp.concatenate([x_ref[c, :, v], y_ref[c, :, v]], axis=1)
            got = lax.dot_general(
                x_ref[c, :, u],
                right,
                (((0,), (0,)), ((), ())),
                preferred_element_type=jnp.float32,
            )
            got = got * scale
            out[0, c, n] = got[:, :TB]
            out[1, c, n] = got[:, TB:]


def correlate(x, tile_pairs):
    cd, rows, inputs = x.shape
    time = rows // 2
    listed = tile_pairs.shape[0]
    rotated = jnp.concatenate([-x[:, time:], x[:, :time]], axis=1)
    step = math.gcd(cd, 2)
    return pl.pallas_call(
        functools.partial(correlate_kernel, 1.0 / time),
        out_shape=jax.ShapeDtypeStruct((2, cd, listed, TB, TB), jnp.float32),
        grid=(cd // step,),
        in_specs=[
            pl.BlockSpec(memory_space=pltpu.SMEM),
            pl.BlockSpec((step, rows, inputs), lambda i: (i, 0, 0)),
            pl.BlockSpec((step, rows, inputs), lambda i: (i, 0, 0)),
        ],
        out_specs=pl.BlockSpec((2, step, listed, TB, TB), lambda i: (0, i, 0, 0, 0)),
        cost_estimate=pl.CostEstimate(
            flops=4 * cd * listed * rows * TB * TB,
            bytes_accessed=8 * cd * listed * TB * TB,
            transcendentals=0,
        ),
        compiler_params=pltpu.CompilerParams(vmem_limit_bytes=40 * 2**20),
    )(tile_pairs, x, rotated)


def on_device(voltages, taps, beam_weights, station_masks, tile_pairs):
    taps_count, channels = taps.shape
    n = lax.axis_size("chan")
    tiles = lax.axis_size("tile")
    total_time = voltages.shape[2] // channels - taps_count + 1
    tile_index = lax.axis_index("tile")
    cd = channels // n
    aligned = tiles == 4 and (2 * cd) % 16 == 0 and voltages.shape[1] % 128 == 0
    if TURN_KERNEL and aligned:
        x = turn(voltages, taps, total_time)
    else:
        spectra = filterbank(voltages, taps, total_time)
        turned = lax.all_to_all(spectra, "chan", split_axis=0, concat_axis=3, tiled=True)
        x = turned.reshape(cd, 2 * total_time, turned.shape[3])
    part = beamform(x, beam_weights, station_masks, tile_index)
    part = jnp.transpose(part, (1, 2, 3, 0)).astype(jnp.bfloat16)
    beams = lax.all_to_all(part, "chan", split_axis=2, concat_axis=3, tiled=True)
    visibility = correlate(x, tile_pairs)
    return (visibility, beams)


def solution(mesh):
    in_specs = (P(None, "chan", None), P(), P(None, "chan", None, None), P(), P("tile", None))
    out_specs = (P(None, "chan", "tile", None, None), P(None, "tile", "chan", None))
    return jax.shard_map(
        on_device, mesh=mesh, in_specs=in_specs, out_specs=out_specs, check_vma=False
    )
```

time: 126 us -> 82.3 us (0.65)
  local copies, waits for them, and re-layouts: 48.9 us -> 14.4 us
  Pallas kernels: 0 us -> 18.9 us
  matrix products: 29.9 us -> 11.3 us
  other arithmetic: 5.54 us -> 0.94 us
  starting transfers between devices: 14.2 us -> 10.8 us
    unnamed x10 -> x8, local copies, waits for them, and re-layouts: 42 us -> 7.75 us
    pallas_call x0 -> x2, Pallas kernels: none -> 18.9 us  [the longest x1 16.9 us: correlate(): pl.pallas_call(functools.partial(correlate_kernel, 1.0 / time), out_shape...]
    dot_general x3 -> x1, matrix products: 29.9 us -> 11.3 us  [filterbank(): jnp.einsum('csrk,ritk->csti', jnp.asarray(dft_table(channels)), frames, p...]
    all_to_all x3 -> x2, starting transfers between devices: 14.2 us -> 10.8 us  [the longest x1 7.25 us: on_device(): lax.all_to_all(spectra, 'chan', split_axis=0, concat_axis=3, tiled=True)]
    another operation x3 -> x0, other arithmetic: 2.54 us -> none  [the longest x2 1.43 us: correlate(): stacked = jnp.stack([left_rows, rotated], axis=0)]
    convert_element_type x1, local copies, waits for them, and re-layouts: 1.65 us -> 3.71 us  [filterbank(): return spectra.astype(jnp.bfloat16)]
    gather x2 -> x0, local copies, waits for them, and re-layouts: 1.98 us -> none  [the longest x1 1 us: correlate(): right_rows = jnp.take(blocks, tile_pairs[:, 1], axis=2)]
    sin x1 -> x0, other arithmetic: 1.73 us -> none  [dft_table(): sine_part = jnp.sin(phases)]
  transfers between devices with their start and end apart: 3 -> 2, of which waited for: 2 -> 1; matrix products, arithmetic and copies ran while one was open for 46% -> 2% of each run, Pallas kernels for 0% -> 21%
where the time goes in v1:
time: 82.3 us; the launch traced here: 81.7 us
  waiting for transfers between devices  24.5 us (30%)
  Pallas kernels  18.9 us (23%)
  local copies, waits for them, and re-layouts  14.4 us (17%)
  matrix products  11.3 us (14%)
  starting transfers between devices  10.8 us (13%)
  other arithmetic  0.94 us (1%)
    all_to_all x1, waiting for transfers between devices, on_device(): lax.all_to_all(spectra, 'chan', split_axis=0, concat_axis=3, tiled=True)  24.5 us
    pallas_call x1, Pallas kernels, correlate(): pl.pallas_call(functools.partial(correlate_kernel, 1.0 / time), out_shape...  16.9 us
    dot_general x1, matrix products, filterbank(): jnp.einsum('csrk,ritk->csti', jnp.asarray(dft_table(channels)), frames, p...  11.3 us
    unnamed x8, local copies, waits for them, and re-layouts  7.75 us
    all_to_all x1, starting transfers between devices, on_device(): lax.all_to_all(spectra, 'chan', split_axis=0, concat_axis=3, tiled=True)  7.25 us
    convert_element_type x1, local copies, waits for them, and re-layouts, filterbank(): return spectra.astype(jnp.bfloat16)  3.71 us
    all_to_all x1, starting transfers between devices, on_device(): lax.all_to_all(part, 'chan', split_axis=2, concat_axis=3, tiled=True)  3.59 us
    pallas_call x1, Pallas kernels, beamform(): pl.pallas_call(functools.partial(beam_kernel, rows // 2), out_shape=jax.S...  2.02 us
  transfers between devices with their start and end apart: 2, of which 1 were waited for; matrix products, arithmetic and copies ran while one was open for 2% of the time, Pallas kernels for 21%

profile of v1, /device:TPU:0, one launch (start us, length us, event | category | flops | bytes accessed | tf_op | source)
XLA Modules:
  0.0 81.7 jit_solution(12322799354383325806)
XLA Ops:
  0.6 1.1 %fusion.7 = (f32[1,256]{1,0:T(1,128)S(1)}, f32[1,256]{1,0:T(1,128)S(1)}, f32[1,256]{1,0:T(1,128)S(1)}, f32[1,256]{1,0:T(1,128)S(1)}, f32[1,256]{1,0:T(1,128)S(1)...) fusion(f32[16,256]{1,0:T(8,128)} %param.7), kind=kLoop, calls=%fused_computation.10 | loop fusion | bytes 32768 | tf_op jit(solution)/shard_map/slice | solution.py:32
  1.7 3.5 %copy.35 = bf16[2,128,5888]{1,2,0:T(8,128)(2,1)S(1)} copy(bf16[2,128,5888]{2,1,0:T(8,128)(2,1)} %param.6) | data formatting | bytes 6029312 | tf_op args[0]
  5.1 11.3 %fusion.4 = bf16[256,2,8,128]{0,3,1,2:T(8,128)(2,1)} fusion(f32[256,2,2,256,1]{3,0,2,1,4:T(8,128)} %constant.14, bf16[2,128,23,256]{1,3,2,0:T(8,128)(2,1)S(1)} %bitcast.49, f32[256]{0:T(256)S(1)} %bitcast.68, f32[256]{0:T(256)S(1)} %bitcast.69, f32[256]{0:T(256)S(1)} %bitcast.55, f32[256]{0:T(256)S(1)} %bitcast.56, f32[256]{0:T(256)S(1)} %bitcast.57, ...), kind=kOutput, calls=%fused_computation.4 | convolution fusion | flops 3246391296 | bytes 18890752 | tf_op jit(solution)/shard_map/csrk,ritk->csti/dot_general | solution.py:33
  16.5 3.7 %copy.37 = bf16[256,2,8,128]{3,1,2,0:T(2,128)(2,1)} copy(bf16[256,2,8,128]{0,3,1,2:T(8,128)(2,1)} %fusion.4) | data formatting | bytes 2097152 | tf_op jit(solution)/shard_map/convert_element_type | solution.py:40
  20.2 7.3 %all-to-all-start = ((bf16[256,2,8,128]{3,1,2,0:T(2,128)(2,1)}), bf16[256,2,8,128]{3,1,2,0:T(2,128)(2,1)S(1)}, u32[]{:S(2)}, u32[]{:S(2)}) async-start(bf16[256,2,8,128]{3,1,2,0:T(2,128)(2,1)} %copy.37), calls=%async_computation | async-start | bytes 2097152 | tf_op jit(solution)/shard_map/all_to_all | solution.py:268
  27.5 0.1 copy.40.pairs
  27.5 0.8 dynamic-slice_convert_fusion
  28.3 0.1 copy.41
  28.4 0.1 broadcast_in_dim.7
  28.6 0.1 copy.42.mask_ref
  28.7 24.5 %all-to-all-done = bf16[256,2,8,128]{3,1,2,0:T(2,128)(2,1)S(1)} async-done(((bf16[256,2,8,128]{3,1,2,0:T(2,128)(2,1)}), bf16[256,2,8,128]{3,1,2,0:T(2,128)(2,1)S(1)}, u32[]{:S(2)}, u32[]{:S(2)}) %all-to-all-start) | async-done | bytes 1048608 | tf_op jit(solution)/shard_map/all_to_all | solution.py:268
  53.2 0.1 copy.38
  53.4 0.3 copy.57
  53.7 0.1 slice_negate_fusion
  53.7 0.0 copy-start
  53.7 3.4 %copy-done = bf16[2,32,64,1024]{3,2,1,0:T(8,128)(2,1)S(1)} copy-done((bf16[2,32,64,1024]{3,2,1,0:T(8,128)(2,1)S(1)}, bf16[2,32,64,1024]{3,2,1,0:T(8,128)(2,1)}, u32[]{:S(2)}) %copy-start) | copy-done | bytes 8388632
  57.1 2.0 %shard_map.78 = f32[32,2,16,8]{3,2,1,0:T(8,128)S(1)} custom-call(s32[1]{0:T(128)} %bitcast.25.where, bf16[2,32,64,1024]{3,2,1,0:T(8,128)(2,1)S(1)} %copy-done, bf16[16,1024]{1,0:T(8,128)(2,1)S(1)} %copy.42.mask_ref, bf16[32,16,1024]{2,1,0:T(8,128)(2,1)S(1)} %bitcast.46), custom_call_target="tpu_custom_call" | custom-call | tf_op jit(solution)/shard_map/pallas_call | solution.py:197
  59.2 0.4 copy.43
  59.6 0.7 reshape.37
  60.3 3.6 %all-to-all-start.1 = ((bf16[8,2,512]{2,1,0:T(2,128)(2,1)}), bf16[8,2,512]{2,1,0:T(2,128)(2,1)S(1)}, u32[]{:S(2)}, u32[]{:S(2)}) async-start(bf16[8,2,512]{2,1,0:T(2,128)(2,1)} %reshape.37), calls=%async_computation.1 | async-start | bytes 32768 | tf_op jit(solution)/shard_map/all_to_all | solution.py:272
  63.9 0.1 pad_maximum_fusion.y_ref
  64.0 16.9 %shard_map.77 = f32[2,32,9,128,128]{4,3,2,1,0:T(8,128)} custom-call(s32[9,2]{1,0:T(8,128)S(1)} %copy.40.pairs, bf16[32,16,1024]{2,1,0:T(8,128)(2,1)S(1)} %bitcast.47, bf16[32,16,1024]{2,1,0:T(8,128)(2,1)S(1)} %pad_maximum_fusion.y_ref), custom_call_target="tpu_custom_call" | custom-call | flops 301989888 | bytes 37748736 | tf_op jit(solution)/shard_map/pallas_call | solution.py:237
  80.9 0.1 reshape.38
  81.0 0.7 all_to_all.24
  (5 shorter events, 0.1 us)
Async XLA Ops:
  16.5 11.0 %copy-start.1 = (s32[9,2]{0,1:T(2,128)S(1)}, s32[9,2]{0,1:T(2,128)}, u32[]{:S(2)}) copy-start(s32[9,2]{0,1:T(2,128)} %param.10) | copy-start | bytes 220
  20.2 33.0 %all-to-all-start = ((bf16[256,2,8,128]{3,1,2,0:T(2,128)(2,1)}), bf16[256,2,8,128]{3,1,2,0:T(2,128)(2,1)S(1)}, u32[]{:S(2)}, u32[]{:S(2)}) async-start(bf16[256,2,8,128]{3,1,2,0:T(2,128)(2,1)} %copy.37), calls=%async_computation | async-start | bytes 2097152 | tf_op jit(solution)/shard_map/all_to_all | solution.py:268
  53.7 3.4 %copy-start = (bf16[2,32,64,1024]{3,2,1,0:T(8,128)(2,1)S(1)}, bf16[2,32,64,1024]{3,2,1,0:T(8,128)(2,1)}, u32[]{:S(2)}) copy-start(bf16[2,32,64,1024]{3,2,1,0:T(8,128)(2,1)} %w_ref.1) | copy-start | bytes 25165828
  60.3 20.6 %all-to-all-start.1 = ((bf16[8,2,512]{2,1,0:T(2,128)(2,1)}), bf16[8,2,512]{2,1,0:T(2,128)(2,1)S(1)}, u32[]{:S(2)}, u32[]{:S(2)}) async-start(bf16[8,2,512]{2,1,0:T(2,128)(2,1)} %reshape.37), calls=%async_computation.1 | async-start | bytes 32768 | tf_op jit(solution)/shard_map/all_to_all | solution.py:272

commit v2 on v1

--- a/solution.py
+++ b/solution.py
@@ -11,7 +11,7 @@
 
 TB = 128
 MESH = pl.DeviceIdType.MESH
-TURN_KERNEL = False
+TURN_KERNEL = True
 
 
 def dft_table(channels):

time: 82.3 us -> 55.3 us (0.67)
  waiting for transfers between devices: 24.5 us -> 0.01 us
  Pallas kernels: 18.9 us -> 36.6 us
  matrix products: 11.3 us -> 0 us
  starting transfers between devices: 10.8 us -> 4.96 us
  local copies, waits for them, and re-layouts: 14.4 us -> 11.6 us
    all_to_all x1 -> x0, waiting for transfers between devices: 24.5 us -> none  [on_device(): lax.all_to_all(spectra, 'chan', split_axis=0, concat_axis=3, tiled=True)]
    pallas_call x0 -> x1, Pallas kernels: none -> 17.7 us  [turn(): pl.pallas_call(functools.partial(turn_kernel, n, tq), out_shape=jax.Shape...]
    dot_general x1 -> x0, matrix products: 11.3 us -> none  [filterbank(): jnp.einsum('csrk,ritk->csti', jnp.asarray(dft_table(channels)), frames, p...]
    all_to_all x1 -> x0, starting transfers between devices: 7.25 us -> none  [on_device(): lax.all_to_all(spectra, 'chan', split_axis=0, concat_axis=3, tiled=True)]
    convert_element_type x1 -> x0, local copies, waits for them, and re-layouts: 3.71 us -> none  [filterbank(): return spectra.astype(jnp.bfloat16)]
    all_to_all x1, starting transfers between devices: 3.59 us -> 4.96 us  [on_device(): lax.all_to_all(part, 'chan', split_axis=2, concat_axis=3, tiled=True)]
    unnamed x8 -> x15, local copies, waits for them, and re-layouts: 7.75 us -> 8.96 us
    reshape x0 -> x2, local copies, waits for them, and re-layouts: none -> 1.17 us  [the longest x1 0.68 us: turn(): got = got.reshape(n, tiles, tq, 2, cd, width).transpose(4, 3, 1, 2, 0, 5)]
  transfers between devices with their start and end apart: 2 -> 1, of which waited for: 1 -> 0; matrix products, arithmetic and copies ran while one was open for 2% -> 0% of each run, Pallas kernels for 21% -> 31%
where the time goes in v2:
time: 55.3 us; the launch traced here: 54.9 us
  Pallas kernels  36.6 us (66%)
  local copies, waits for them, and re-layouts  11.6 us (21%)
  starting transfers between devices  4.96 us (9%)
  other arithmetic  0.96 us (2%)
  between operations  0.74 us (1%)
    pallas_call x1, Pallas kernels, turn(): pl.pallas_call(functools.partial(turn_kernel, n, tq), out_shape=jax.Shape...  17.7 us
    pallas_call x1, Pallas kernels, correlate(): pl.pallas_call(functools.partial(correlate_kernel, 1.0 / time), out_shape...  16.9 us
    unnamed x15, local copies, waits for them, and re-layouts  8.96 us
    all_to_all x1, starting transfers between devices, on_device(): lax.all_to_all(part, 'chan', split_axis=2, concat_axis=3, tiled=True)  4.96 us
    pallas_call x1, Pallas kernels, beamform(): pl.pallas_call(functools.partial(beam_kernel, rows // 2), out_shape=jax.S...  2.02 us
  transfers between devices with their start and end apart: 1, of which 0 were waited for; matrix products, arithmetic and copies ran while one was open for 0% of the time, Pallas kernels for 31%

profile of v2, /device:TPU:0, one launch (start us, length us, event | category | flops | bytes accessed | tf_op | source)
XLA Modules:
  0.0 54.9 jit_solution(1298847074644576005)
XLA Ops:
  0.6 1.8 %copy-done.1 = bf16[2,128,5888]{2,1,0:T(8,128)(2,1)S(1)} copy-done((bf16[2,128,5888]{2,1,0:T(8,128)(2,1)S(1)}, bf16[2,128,5888]{2,1,0:T(8,128)(2,1)}, u32[]{:S(2)}) %copy-start.1) | copy-done | bytes 3014680
  2.5 1.0 %copy-done.2 = bf16[512,512]{1,0:T(8,128)(2,1)S(1)} copy-done((bf16[512,512]{1,0:T(8,128)(2,1)S(1)}, bf16[512,512]{1,0:T(8,128)(2,1)}, u32[]{:S(2)}) %copy-start.2) | copy-done | bytes 524312
  3.5 1.0 %copy-done.3 = bf16[512,512]{1,0:T(8,128)(2,1)S(1)} copy-done((bf16[512,512]{1,0:T(8,128)(2,1)S(1)}, bf16[512,512]{1,0:T(8,128)(2,1)}, u32[]{:S(2)}) %copy-start.3) | copy-done | bytes 524312
  4.6 0.7 %copy-done.4 = f32[16,256]{1,0:T(8,128)S(1)} copy-done((f32[16,256]{1,0:T(8,128)S(1)}, f32[16,256]{1,0:T(8,128)}, u32[]{:S(2)}) %copy-start.4) | copy-done | bytes 16408
  5.3 17.7 %shard_map.86 = bf16[8,4,128,128]{3,2,1,0:T(8,128)(2,1)S(1)} custom-call(bf16[2,128,5888]{2,1,0:T(8,128)(2,1)S(1)} %copy-done.1, f32[16,256]{1,0:T(8,128)S(1)} %copy-done.4, bf16[512,512]{1,0:T(8,128)(2,1)S(1)} %copy-done.2, bf16[512,512]{1,0:T(8,128)(2,1)S(1)} %copy-done.3), custom_call_target="tpu_custom_call" | custom-call | tf_op jit(solution)/shard_map/pallas_call | solution.py:159
  23.0 0.7 %copy.25 = bf16[8,4,2,2,32,128]{5,0,2,1,3,4:T(8,128)(2,1)S(1)} copy(bf16[8,4,2,2,32,128]{5,4,3,2,1,0:T(8,128)(2,1)S(1)} %bitcast.15) | data formatting | bytes 2097152 | tf_op jit(solution)/shard_map/reshape | solution.py:169
  23.7 0.5 reshape.16.x_ref
  24.2 0.8 %dynamic-slice_convert_fusion = bf16[16,512]{1,0:T(8,128)(2,1)S(1)} fusion(s32[64,512]{1,0:T(8,128)} %param.10, s32[]{:T(128)S(6)} %select_n.3), kind=kLoop, calls=%fused_computation.4 | loop fusion | flops 8192 | bytes 49156 | tf_op jit(solution)/shard_map/convert_element_type | solution.py:195
  24.9 0.1 copy.19
  25.1 0.1 broadcast_in_dim.7
  25.2 0.1 copy.20.mask_ref
  25.3 3.4 %copy-done = bf16[2,32,64,1024]{3,2,1,0:T(8,128)(2,1)S(1)} copy-done((bf16[2,32,64,1024]{3,2,1,0:T(8,128)(2,1)S(1)}, bf16[2,32,64,1024]{3,2,1,0:T(8,128)(2,1)}, u32[]{:S(2)}) %copy-start) | copy-done | bytes 8388632
  28.7 2.0 %shard_map.88 = f32[32,2,16,8]{3,2,1,0:T(8,128)S(1)} custom-call(s32[1]{0:T(128)} %bitcast.2.where, bf16[2,32,64,1024]{3,2,1,0:T(8,128)(2,1)S(1)} %copy-done, bf16[16,1024]{1,0:T(8,128)(2,1)S(1)} %copy.20.mask_ref, bf16[32,16,1024]{2,1,0:T(8,128)(2,1)S(1)} %reshape.16.x_ref), custom_call_target="tpu_custom_call" | custom-call | tf_op jit(solution)/shard_map/pallas_call | solution.py:197
  30.8 0.4 copy.21
  31.2 0.7 %reshape.17 = bf16[8,2,512]{2,1,0:T(2,128)(2,1)} reshape(bf16[8,2,16,32]{3,2,1,0:T(8,128)(2,1)S(1)} %bitcast.18) | data formatting | bytes 32768
  31.9 5.0 %all-to-all-start = ((bf16[8,2,512]{2,1,0:T(2,128)(2,1)}), bf16[8,2,512]{2,1,0:T(2,128)(2,1)S(1)}, u32[]{:S(2)}, u32[]{:S(2)}) async-start(bf16[8,2,512]{2,1,0:T(2,128)(2,1)} %reshape.17), calls=%async_computation | async-start | bytes 32768 | tf_op jit(solution)/shard_map/all_to_all | solution.py:272
  36.8 0.1 slice_negate_fusion
  36.9 0.1 pad_maximum_fusion.y_ref
  37.0 0.0 copy-done.5
  37.0 0.1 copy.18.pairs
  37.1 16.9 %shard_map.87 = f32[2,32,9,128,128]{4,3,2,1,0:T(8,128)} custom-call(s32[9,2]{1,0:T(8,128)S(1)} %copy.18.pairs, bf16[32,16,1024]{2,1,0:T(8,128)(2,1)S(1)} %reshape.16.x_ref, bf16[32,16,1024]{2,1,0:T(8,128)(2,1)S(1)} %pad_maximum_fusion.y_ref), custom_call_target="tpu_custom_call" | custom-call | flops 301989888 | bytes 37748736 | tf_op jit(solution)/shard_map/pallas_call | solution.py:237
  54.0 0.0 all-to-all-done
  54.0 0.1 reshape.18
  54.1 0.7 %all_to_all.10 = bf16[2,16,1,256]{3,1,0,2:T(8,128)(2,1)} reshape(bf16[2,16,8,32]{3,2,1,0:T(8,128)(2,1)S(1)} %copy.22) | data formatting | bytes 32768 | tf_op jit(solution)/shard_map/all_to_all | solution.py:272
  (8 shorter events, 0.1 us)
Async XLA Ops:
  0.6 1.9 %copy-start.1 = (bf16[2,128,5888]{2,1,0:T(8,128)(2,1)S(1)}, bf16[2,128,5888]{2,1,0:T(8,128)(2,1)}, u32[]{:S(2)}) copy-start(bf16[2,128,5888]{2,1,0:T(8,128)(2,1)} %volts.1) | copy-start | bytes 9043972
  2.5 1.0 %copy-start.2 = (bf16[512,512]{1,0:T(8,128)(2,1)S(1)}, bf16[512,512]{1,0:T(8,128)(2,1)}, u32[]{:S(2)}) copy-start(bf16[512,512]{1,0:T(8,128)(2,1)} %constant.14.clone.hi_ref) | copy-start | bytes 1572868
  3.5 1.0 %copy-start.3 = (bf16[512,512]{1,0:T(8,128)(2,1)S(1)}, bf16[512,512]{1,0:T(8,128)(2,1)}, u32[]{:S(2)}) copy-start(bf16[512,512]{1,0:T(8,128)(2,1)} %constant.15.clone.lo_ref) | copy-start | bytes 1572868
  4.6 0.7 %copy-start.4 = (f32[16,256]{1,0:T(8,128)S(1)}, f32[16,256]{1,0:T(8,128)}, u32[]{:S(2)}) copy-start(f32[16,256]{1,0:T(8,128)} %taps_ref.1) | copy-start | bytes 49156
  25.3 3.4 %copy-start = (bf16[2,32,64,1024]{3,2,1,0:T(8,128)(2,1)S(1)}, bf16[2,32,64,1024]{3,2,1,0:T(8,128)(2,1)}, u32[]{:S(2)}) copy-start(bf16[2,32,64,1024]{3,2,1,0:T(8,128)(2,1)} %w_ref.1) | copy-start | bytes 25165828
  30.7 6.3 %copy-start.5 = (s32[9,2]{0,1:T(2,128)S(1)}, s32[9,2]{0,1:T(2,128)}, u32[]{:S(2)}) copy-start(s32[9,2]{0,1:T(2,128)} %param.11) | copy-start | bytes 220
  31.9 22.1 %all-to-all-start = ((bf16[8,2,512]{2,1,0:T(2,128)(2,1)}), bf16[8,2,512]{2,1,0:T(2,128)(2,1)S(1)}, u32[]{:S(2)}, u32[]{:S(2)}) async-start(bf16[8,2,512]{2,1,0:T(2,128)(2,1)} %reshape.17), calls=%async_computation | async-start | bytes 32768 | tf_op jit(solution)/shard_map/all_to_all | solution.py:272

commit v3 on v2

--- a/solution.py
+++ b/solution.py
@@ -207,23 +207,28 @@
             ],
             out_specs=pl.BlockSpec((step, 2, beams, rows // 2), lambda i, at: (i, 0, 0, 0)),
         ),
-        compiler_params=pltpu.CompilerParams(vmem_limit_bytes=40 * 2**20),
+        compiler_params=pltpu.CompilerParams(vmem_limit_bytes=54 * 2**20),
     )(tile_index[None].astype(jnp.int32), beam_weights, live, x)
 
 
-def correlate_kernel(scale, pairs, x_ref, y_ref, out):
+def correlate_kernel(time, pairs, x_ref, y_ref, out):
+    exact = time & (time - 1) == 0
+    scale = 1.0 / time
     for c in range(x_ref.shape[0]):
+        sides = []
         for n in range(out.shape[2]):
             u = pl.ds(pl.multiple_of(pairs[n, 0] * TB, TB), TB)
             v = pl.ds(pl.multiple_of(pairs[n, 1] * TB, TB), TB)
-            right = jnp.concatenate([x_ref[c, :, v], y_ref[c, :, v]], axis=1)
+            left = x_ref[c, :, u]
+            if exact:
+                left = left * jnp.asarray(scale, left.dtype)
+            sides.append((left, jnp.concatenate([x_ref[c, :, v], y_ref[c, :, v]], axis=1)))
+        for n, (left, right) in enumerate(sides):
             got = lax.dot_general(
-                x_ref[c, :, u],
-                right,
-                (((0,), (0,)), ((), ())),
-                preferred_element_type=jnp.float32,
+                left, right, (((0,), (0,)), ((), ())), preferred_element_type=jnp.float32
             )
-            got = got * scale
+            if not exact:
+                got = got * scale
             out[0, c, n] = got[:, :TB]
             out[1, c, n] = got[:, TB:]
 
@@ -235,7 +240,7 @@
     rotated = jnp.concatenate([-x[:, time:], x[:, :time]], axis=1)
     step = math.gcd(cd, 2)
     return pl.pallas_call(
-        functools.partial(correlate_kernel, 1.0 / time),
+        functools.partial(correlate_kernel, time),
         out_shape=jax.ShapeDtypeStruct((2, cd, listed, TB, TB), jnp.float32),
         grid=(cd // step,),
         in_specs=[

time: 55.3 us -> 57 us (1.031)
  Pallas kernels: 36.6 us -> 39.1 us
  local copies, waits for them, and re-layouts: 11.6 us -> 9.62 us
  other arithmetic: 0.96 us -> 2.01 us
    unnamed x15, local copies, waits for them, and re-layouts: 8.96 us -> 5.57 us
    pallas_call x1, Pallas kernels: 2.02 us -> 4.59 us  [beamform(): pl.pallas_call(functools.partial(beam_kernel, rows // 2), out_shape=jax.S...]
    convert_element_type x1, other arithmetic: 0.04 us -> 1.09 us  [on_device(): part = jnp.transpose(part, (1, 2, 3, 0)).astype(jnp.bfloat16)]
    reshape x1, local copies, waits for them, and re-layouts: 0.49 us -> 1.27 us  [turn(): return got.reshape(cd, 2 * total_time, n * width)]
    convert_element_type x2, local copies, waits for them, and re-layouts: 0.23 us -> 0.85 us  [beamform(): live = jnp.repeat(own, 2, axis=1).astype(jnp.bfloat16)]
  transfers between devices with their start and end apart: 1 -> 1, of which waited for: 0 -> 0; matrix products, arithmetic and copies ran while one was open for 0% -> 0% of each run, Pallas kernels for 31% -> 30%
where the time goes in v3:
time: 57 us; the launch traced here: 56.5 us
  Pallas kernels  39.1 us (69%)
  local copies, waits for them, and re-layouts  9.62 us (17%)
  starting transfers between devices  4.96 us (9%)
  other arithmetic  2.01 us (4%)
  between operations  0.72 us (1%)
    pallas_call x1, Pallas kernels, turn(): pl.pallas_call(functools.partial(turn_kernel, n, tq), out_shape=jax.Shape...  17.7 us
    pallas_call x1, Pallas kernels, correlate(): pl.pallas_call(functools.partial(correlate_kernel, time), out_shape=jax.S...  16.9 us
    unnamed x15, local copies, waits for them, and re-layouts  5.57 us
    all_to_all x1, starting transfers between devices, on_device(): lax.all_to_all(part, 'chan', split_axis=2, concat_axis=3, tiled=True)  4.96 us
    pallas_call x1, Pallas kernels, beamform(): pl.pallas_call(functools.partial(beam_kernel, rows // 2), out_shape=jax.S...  4.59 us
    reshape x1, local copies, waits for them, and re-layouts, turn(): return got.reshape(cd, 2 * total_time, n * width)  1.27 us
  transfers between devices with their start and end apart: 1, of which 0 were waited for; matrix products, arithmetic and copies ran while one was open for 0% of the time, Pallas kernels for 30%

profile of v3, /device:TPU:0, one launch (start us, length us, event | category | flops | bytes accessed | tf_op | source)
XLA Modules:
  0.0 56.5 jit_solution(2735907598833954527)
XLA Ops:
  0.6 0.0 copy-start.1
  0.6 1.8 %copy-done.1 = bf16[2,128,5888]{2,1,0:T(8,128)(2,1)S(1)} copy-done((bf16[2,128,5888]{2,1,0:T(8,128)(2,1)S(1)}, bf16[2,128,5888]{2,1,0:T(8,128)(2,1)}, u32[]{:S(2)}) %copy-start.1) | copy-done | bytes 3014680
  2.5 1.0 %copy-done.2 = bf16[512,512]{1,0:T(8,128)(2,1)S(1)} copy-done((bf16[512,512]{1,0:T(8,128)(2,1)S(1)}, bf16[512,512]{1,0:T(8,128)(2,1)}, u32[]{:S(2)}) %copy-start.2) | copy-done | bytes 524312
  3.5 1.0 %copy-done.3 = bf16[512,512]{1,0:T(8,128)(2,1)S(1)} copy-done((bf16[512,512]{1,0:T(8,128)(2,1)S(1)}, bf16[512,512]{1,0:T(8,128)(2,1)}, u32[]{:S(2)}) %copy-start.3) | copy-done | bytes 524312
  4.6 0.7 %copy-done.4 = f32[16,256]{1,0:T(8,128)S(1)} copy-done((f32[16,256]{1,0:T(8,128)S(1)}, f32[16,256]{1,0:T(8,128)}, u32[]{:S(2)}) %copy-start.4) | copy-done | bytes 16408
  5.3 17.7 %shard_map.86 = bf16[8,4,128,128]{3,2,1,0:T(8,128)(2,1)S(1)} custom-call(bf16[2,128,5888]{2,1,0:T(8,128)(2,1)S(1)} %copy-done.1, f32[16,256]{1,0:T(8,128)S(1)} %copy-done.4, bf16[512,512]{1,0:T(8,128)(2,1)S(1)} %copy-done.2, bf16[512,512]{1,0:T(8,128)(2,1)S(1)} %copy-done.3), custom_call_target="tpu_custom_call" | custom-call | tf_op jit(solution)/shard_map/pallas_call | solution.py:159
  23.0 0.7 %copy.25 = bf16[8,4,2,2,32,128]{5,0,2,1,3,4:T(8,128)(2,1)S(1)} copy(bf16[8,4,2,2,32,128]{5,4,3,2,1,0:T(8,128)(2,1)S(1)} %bitcast.15) | data formatting | bytes 2097152 | tf_op jit(solution)/shard_map/reshape | solution.py:169
  23.7 1.3 %reshape.16.x_ref = bf16[32,16,1024]{2,1,0:T(8,128)(2,1)} reshape(bf16[32,2,4,2,8,128]{5,4,3,2,1,0:T(8,128)(2,1)S(1)} %bitcast.16) | data formatting | bytes 2097152 | tf_op jit(solution)/shard_map/reshape | solution.py:170
  24.9 0.8 %dynamic-slice_convert_fusion = bf16[16,512]{1,0:T(8,128)(2,1)S(1)} fusion(s32[64,512]{1,0:T(8,128)} %param.10, s32[]{:T(128)S(6)} %select_n.3), kind=kLoop, calls=%fused_computation.4 | loop fusion | flops 8192 | bytes 49156 | tf_op jit(solution)/shard_map/convert_element_type | solution.py:195
  25.7 0.1 copy.19
  25.8 0.1 broadcast_in_dim.7
  26.0 0.7 %copy.20.mask_ref = bf16[16,1024]{1,0:T(8,128)(2,1)} copy(bf16[16,1024]{0,1:T(8,128)(2,1)S(1)} %bitcast.17) | data formatting | bytes 65536 | tf_op jit(solution)/shard_map/convert_element_type | solution.py:195
  26.7 4.6 %shard_map.88 = f32[32,2,16,8]{3,2,1,0:T(8,128)} custom-call(s32[1]{0:T(128)} %bitcast.2.where, bf16[2,32,64,1024]{3,2,1,0:T(8,128)(2,1)} %w_ref.1, bf16[16,1024]{1,0:T(8,128)(2,1)} %copy.20.mask_ref, bf16[32,16,1024]{2,1,0:T(8,128)(2,1)} %reshape.16.x_ref), custom_call_target="tpu_custom_call" | custom-call | tf_op jit(solution)/shard_map/pallas_call | solution.py:197
  31.3 1.1 %convert_bitcast_fusion = bf16[2,16,8,32]{2,1,0,3:T(8,128)(2,1)S(1)} fusion(f32[32,2,16,8]{3,2,1,0:T(8,128)} %shard_map.88), kind=kLoop, calls=%fused_computation.3 | loop fusion | flops 8192 | bytes 49152 | tf_op jit(solution)/shard_map/convert_element_type | solution.py:276
  32.4 0.4 copy.21
  32.8 0.7 %reshape.17 = bf16[8,2,512]{2,1,0:T(2,128)(2,1)} reshape(bf16[8,2,16,32]{3,2,1,0:T(8,128)(2,1)S(1)} %bitcast.18) | data formatting | bytes 32768
  33.5 5.0 %all-to-all-start = ((bf16[8,2,512]{2,1,0:T(2,128)(2,1)}), bf16[8,2,512]{2,1,0:T(2,128)(2,1)S(1)}, u32[]{:S(2)}, u32[]{:S(2)}) async-start(bf16[8,2,512]{2,1,0:T(2,128)(2,1)} %reshape.17), calls=%async_computation | async-start | bytes 32768 | tf_op jit(solution)/shard_map/all_to_all | solution.py:277
  38.5 0.1 slice_negate_fusion
  38.5 0.1 pad_maximum_fusion.y_ref
  38.6 0.1 copy.18.pairs
  38.7 16.9 %shard_map.87 = f32[2,32,9,128,128]{4,3,2,1,0:T(8,128)} custom-call(s32[9,2]{1,0:T(8,128)S(1)} %copy.18.pairs, bf16[32,16,1024]{2,1,0:T(8,128)(2,1)S(1)} %copy-done, bf16[32,16,1024]{2,1,0:T(8,128)(2,1)S(1)} %pad_maximum_fusion.y_ref), custom_call_target="tpu_custom_call" | custom-call | flops 301989888 | bytes 37748736 | tf_op jit(solution)/shard_map/pallas_call | solution.py:242
  55.6 0.0 all-to-all-done
  55.6 0.1 reshape.18
  55.8 0.7 %all_to_all.10 = bf16[2,16,1,256]{3,1,0,2:T(8,128)(2,1)} reshape(bf16[2,16,8,32]{3,2,1,0:T(8,128)(2,1)S(1)} %copy.22) | data formatting | bytes 32768 | tf_op jit(solution)/shard_map/all_to_all | solution.py:277
  (8 shorter events, 0.0 us)
Async XLA Ops:
  0.6 1.9 %copy-start.1 = (bf16[2,128,5888]{2,1,0:T(8,128)(2,1)S(1)}, bf16[2,128,5888]{2,1,0:T(8,128)(2,1)}, u32[]{:S(2)}) copy-start(bf16[2,128,5888]{2,1,0:T(8,128)(2,1)} %volts.1) | copy-start | bytes 9043972
  2.5 1.0 %copy-start.2 = (bf16[512,512]{1,0:T(8,128)(2,1)S(1)}, bf16[512,512]{1,0:T(8,128)(2,1)}, u32[]{:S(2)}) copy-start(bf16[512,512]{1,0:T(8,128)(2,1)} %constant.14.clone.hi_ref) | copy-start | bytes 1572868
  3.5 1.0 %copy-start.3 = (bf16[512,512]{1,0:T(8,128)(2,1)S(1)}, bf16[512,512]{1,0:T(8,128)(2,1)}, u32[]{:S(2)}) copy-start(bf16[512,512]{1,0:T(8,128)(2,1)} %constant.15.clone.lo_ref) | copy-start | bytes 1572868
  4.6 0.7 %copy-start.4 = (f32[16,256]{1,0:T(8,128)S(1)}, f32[16,256]{1,0:T(8,128)}, u32[]{:S(2)}) copy-start(f32[16,256]{1,0:T(8,128)} %taps_ref.1) | copy-start | bytes 49156
  26.7 11.8 %copy-start = (bf16[32,16,1024]{2,1,0:T(8,128)(2,1)S(1)}, bf16[32,16,1024]{2,1,0:T(8,128)(2,1)}, u32[]{:S(2)}) copy-start(bf16[32,16,1024]{2,1,0:T(8,128)(2,1)} %reshape.16.x_ref) | copy-start | bytes 3145732
  31.3 7.3 %copy-start.5 = (s32[9,2]{0,1:T(2,128)S(1)}, s32[9,2]{0,1:T(2,128)}, u32[]{:S(2)}) copy-start(s32[9,2]{0,1:T(2,128)} %param.11) | copy-start | bytes 220
  33.5 22.1 %all-to-all-start = ((bf16[8,2,512]{2,1,0:T(2,128)(2,1)}), bf16[8,2,512]{2,1,0:T(2,128)(2,1)S(1)}, u32[]{:S(2)}, u32[]{:S(2)}) async-start(bf16[8,2,512]{2,1,0:T(2,128)(2,1)} %reshape.17), calls=%async_computation | async-start | bytes 32768 | tf_op jit(solution)/shard_map/all_to_all | solution.py:277

commit v4 on v2

--- a/solution.py
+++ b/solution.py
@@ -211,9 +211,30 @@
     )(tile_index[None].astype(jnp.int32), beam_weights, live, x)
 
 
-def correlate_kernel(scale, pairs, x_ref, y_ref, out):
-    for c in range(x_ref.shape[0]):
-        for n in range(out.shape[2]):
+def correlate_kernel(scale, pairs, x_ref, y_ref, out, held, sems):
+    step = x_ref.shape[0]
+    slots = held.shape[0]
+    i = pl.program_id(0)
+    last = pl.num_programs(0) - 1
+
+    def send(at, o, c):
+        slot = lax.rem(at, slots)
+        return pltpu.make_async_copy(
+            held.at[slot, o, c], out.at[o, at * step + c], sems.at[slot, o, c]
+        )
+
+    def finish(at):
+        for c in range(step):
+            for o in range(2):
+                send(at, o, c).wait()
+
+    @pl.when(i >= slots)
+    def _():
+        finish(i - slots)
+
+    slot = lax.rem(i, slots)
+    for c in range(step):
+        for n in range(held.shape[3]):
             u = pl.ds(pl.multiple_of(pairs[n, 0] * TB, TB), TB)
             v = pl.ds(pl.multiple_of(pairs[n, 1] * TB, TB), TB)
             right = jnp.concatenate([x_ref[c, :, v], y_ref[c, :, v]], axis=1)
@@ -224,8 +245,15 @@
                 preferred_element_type=jnp.float32,
             )
             got = got * scale
-            out[0, c, n] = got[:, :TB]
-            out[1, c, n] = got[:, TB:]
+            held[slot, 0, c, n] = got[:, :TB]
+            held[slot, 1, c, n] = got[:, TB:]
+        for o in range(2):
+            send(i, o, c).start()
+
+    @pl.when(i == last)
+    def _():
+        for back in range(slots - 1, -1, -1):
+            finish(i - back)
 
 
 def correlate(x, tile_pairs):
@@ -234,6 +262,7 @@
     listed = tile_pairs.shape[0]
     rotated = jnp.concatenate([-x[:, time:], x[:, :time]], axis=1)
     step = math.gcd(cd, 2)
+    slots = min(4, cd // step)
     return pl.pallas_call(
         functools.partial(correlate_kernel, 1.0 / time),
         out_shape=jax.ShapeDtypeStruct((2, cd, listed, TB, TB), jnp.float32),
@@ -243,7 +272,11 @@
             pl.BlockSpec((step, rows, inputs), lambda i: (i, 0, 0)),
             pl.BlockSpec((step, rows, inputs), lambda i: (i, 0, 0)),
         ],
-        out_specs=pl.BlockSpec((2, step, listed, TB, TB), lambda i: (0, i, 0, 0, 0)),
+        out_specs=pl.BlockSpec(memory_space=pl.ANY),
+        scratch_shapes=[
+            pltpu.VMEM((slots, 2, step, listed, TB, TB), jnp.float32),
+            pltpu.SemaphoreType.DMA((slots, 2, step)),
+        ],
         cost_estimate=pl.CostEstimate(
             flops=4 * cd * listed * rows * TB * TB,
             bytes_accessed=8 * cd * listed * TB * TB,

time: 55.3 us -> 51.8 us (0.937)
  Pallas kernels: 36.6 us -> 33 us
    pallas_call x1, Pallas kernels: 16.9 us -> 13.3 us  [correlate(): pl.pallas_call(functools.partial(correlate_kernel, 1.0 / time), out_shape...]
  transfers between devices with their start and end apart: 1 -> 1, of which waited for: 0 -> 0; matrix products, arithmetic and copies ran while one was open for 0% -> 0% of each run, Pallas kernels for 31% -> 26%
where the time goes in v4:
time: 51.8 us; the launch traced here: 51.3 us
  Pallas kernels  33 us (64%)
  local copies, waits for them, and re-layouts  11.6 us (22%)
  starting transfers between devices  4.96 us (10%)
  other arithmetic  0.96 us (2%)
  between operations  0.75 us (1%)
    pallas_call x1, Pallas kernels, turn(): pl.pallas_call(functools.partial(turn_kernel, n, tq), out_shape=jax.Shape...  17.7 us
    pallas_call x1, Pallas kernels, correlate(): pl.pallas_call(functools.partial(correlate_kernel, 1.0 / time), out_shape...  13.3 us
    unnamed x15, local copies, waits for them, and re-layouts  8.96 us
    all_to_all x1, starting transfers between devices, on_device(): lax.all_to_all(part, 'chan', split_axis=2, concat_axis=3, tiled=True)  4.96 us
    pallas_call x1, Pallas kernels, beamform(): pl.pallas_call(functools.partial(beam_kernel, rows // 2), out_shape=jax.S...  2.02 us
  transfers between devices with their start and end apart: 1, of which 0 were waited for; matrix products, arithmetic and copies ran while one was open for 0% of the time, Pallas kernels for 26%

profile of v4, /device:TPU:0, one launch (start us, length us, event | category | flops | bytes accessed | tf_op | source)
XLA Modules:
  0.0 51.3 jit_solution(13045137237359756305)
XLA Ops:
  0.6 1.8 %copy-done.1 = bf16[2,128,5888]{2,1,0:T(8,128)(2,1)S(1)} copy-done((bf16[2,128,5888]{2,1,0:T(8,128)(2,1)S(1)}, bf16[2,128,5888]{2,1,0:T(8,128)(2,1)}, u32[]{:S(2)}) %copy-start.1) | copy-done | bytes 3014680
  2.5 1.0 %copy-done.2 = bf16[512,512]{1,0:T(8,128)(2,1)S(1)} copy-done((bf16[512,512]{1,0:T(8,128)(2,1)S(1)}, bf16[512,512]{1,0:T(8,128)(2,1)}, u32[]{:S(2)}) %copy-start.2) | copy-done | bytes 524312
  3.5 1.0 %copy-done.3 = bf16[512,512]{1,0:T(8,128)(2,1)S(1)} copy-done((bf16[512,512]{1,0:T(8,128)(2,1)S(1)}, bf16[512,512]{1,0:T(8,128)(2,1)}, u32[]{:S(2)}) %copy-start.3) | copy-done | bytes 524312
  4.6 0.7 %copy-done.4 = f32[16,256]{1,0:T(8,128)S(1)} copy-done((f32[16,256]{1,0:T(8,128)S(1)}, f32[16,256]{1,0:T(8,128)}, u32[]{:S(2)}) %copy-start.4) | copy-done | bytes 16408
  5.3 17.7 %shard_map.86 = bf16[8,4,128,128]{3,2,1,0:T(8,128)(2,1)S(1)} custom-call(bf16[2,128,5888]{2,1,0:T(8,128)(2,1)S(1)} %copy-done.1, f32[16,256]{1,0:T(8,128)S(1)} %copy-done.4, bf16[512,512]{1,0:T(8,128)(2,1)S(1)} %copy-done.2, bf16[512,512]{1,0:T(8,128)(2,1)S(1)} %copy-done.3), custom_call_target="tpu_custom_call" | custom-call | tf_op jit(solution)/shard_map/pallas_call | solution.py:159
  23.0 0.7 %copy.25 = bf16[8,4,2,2,32,128]{5,0,2,1,3,4:T(8,128)(2,1)S(1)} copy(bf16[8,4,2,2,32,128]{5,4,3,2,1,0:T(8,128)(2,1)S(1)} %bitcast.15) | data formatting | bytes 2097152 | tf_op jit(solution)/shard_map/reshape | solution.py:169
  23.7 0.5 reshape.16.x_ref
  24.2 0.8 %dynamic-slice_convert_fusion = bf16[16,512]{1,0:T(8,128)(2,1)S(1)} fusion(s32[64,512]{1,0:T(8,128)} %param.10, s32[]{:T(128)S(6)} %select_n.3), kind=kLoop, calls=%fused_computation.4 | loop fusion | flops 8192 | bytes 49156 | tf_op jit(solution)/shard_map/convert_element_type | solution.py:195
  24.9 0.1 copy.19
  25.1 0.1 broadcast_in_dim.7
  25.2 0.1 copy.20.mask_ref
  25.3 3.4 %copy-done = bf16[2,32,64,1024]{3,2,1,0:T(8,128)(2,1)S(1)} copy-done((bf16[2,32,64,1024]{3,2,1,0:T(8,128)(2,1)S(1)}, bf16[2,32,64,1024]{3,2,1,0:T(8,128)(2,1)}, u32[]{:S(2)}) %copy-start) | copy-done | bytes 8388632
  28.7 2.0 %shard_map.88 = f32[32,2,16,8]{3,2,1,0:T(8,128)S(1)} custom-call(s32[1]{0:T(128)} %bitcast.2.where, bf16[2,32,64,1024]{3,2,1,0:T(8,128)(2,1)S(1)} %copy-done, bf16[16,1024]{1,0:T(8,128)(2,1)S(1)} %copy.20.mask_ref, bf16[32,16,1024]{2,1,0:T(8,128)(2,1)S(1)} %reshape.16.x_ref), custom_call_target="tpu_custom_call" | custom-call | tf_op jit(solution)/shard_map/pallas_call | solution.py:197
  30.8 0.4 copy.21
  31.2 0.7 %reshape.17 = bf16[8,2,512]{2,1,0:T(2,128)(2,1)} reshape(bf16[8,2,16,32]{3,2,1,0:T(8,128)(2,1)S(1)} %bitcast.18) | data formatting | bytes 32768
  31.9 5.0 %all-to-all-start = ((bf16[8,2,512]{2,1,0:T(2,128)(2,1)}), bf16[8,2,512]{2,1,0:T(2,128)(2,1)S(1)}, u32[]{:S(2)}, u32[]{:S(2)}) async-start(bf16[8,2,512]{2,1,0:T(2,128)(2,1)} %reshape.17), calls=%async_computation | async-start | bytes 32768 | tf_op jit(solution)/shard_map/all_to_all | solution.py:305
  36.8 0.1 slice_negate_fusion
  36.9 0.1 pad_maximum_fusion.y_ref
  37.0 0.0 copy-done.5
  37.0 0.1 copy.18.pairs
  37.1 13.3 %shard_map.87 = f32[2,32,9,128,128]{4,3,2,1,0:T(8,128)} custom-call(s32[9,2]{1,0:T(8,128)S(1)} %copy.18.pairs, bf16[32,16,1024]{2,1,0:T(8,128)(2,1)S(1)} %reshape.16.x_ref, bf16[32,16,1024]{2,1,0:T(8,128)(2,1)S(1)} %pad_maximum_fusion.y_ref), custom_call_target="tpu_custom_call" | custom-call | flops 301989888 | bytes 37748736 | tf_op jit(solution)/shard_map/pallas_call | solution.py:266
  50.4 0.0 all-to-all-done
  50.4 0.1 reshape.18
  50.6 0.7 %all_to_all.10 = bf16[2,16,1,256]{3,1,0,2:T(8,128)(2,1)} reshape(bf16[2,16,8,32]{3,2,1,0:T(8,128)(2,1)S(1)} %copy.22) | data formatting | bytes 32768 | tf_op jit(solution)/shard_map/all_to_all | solution.py:305
  (8 shorter events, 0.1 us)
Async XLA Ops:
  0.6 1.9 %copy-start.1 = (bf16[2,128,5888]{2,1,0:T(8,128)(2,1)S(1)}, bf16[2,128,5888]{2,1,0:T(8,128)(2,1)}, u32[]{:S(2)}) copy-start(bf16[2,128,5888]{2,1,0:T(8,128)(2,1)} %volts.1) | copy-start | bytes 9043972
  2.5 1.0 %copy-start.2 = (bf16[512,512]{1,0:T(8,128)(2,1)S(1)}, bf16[512,512]{1,0:T(8,128)(2,1)}, u32[]{:S(2)}) copy-start(bf16[512,512]{1,0:T(8,128)(2,1)} %constant.14.clone.hi_ref) | copy-start | bytes 1572868
  3.5 1.0 %copy-start.3 = (bf16[512,512]{1,0:T(8,128)(2,1)S(1)}, bf16[512,512]{1,0:T(8,128)(2,1)}, u32[]{:S(2)}) copy-start(bf16[512,512]{1,0:T(8,128)(2,1)} %constant.15.clone.lo_ref) | copy-start | bytes 1572868
  4.6 0.7 %copy-start.4 = (f32[16,256]{1,0:T(8,128)S(1)}, f32[16,256]{1,0:T(8,128)}, u32[]{:S(2)}) copy-start(f32[16,256]{1,0:T(8,128)} %taps_ref.1) | copy-start | bytes 49156
  25.3 3.4 %copy-start = (bf16[2,32,64,1024]{3,2,1,0:T(8,128)(2,1)S(1)}, bf16[2,32,64,1024]{3,2,1,0:T(8,128)(2,1)}, u32[]{:S(2)}) copy-start(bf16[2,32,64,1024]{3,2,1,0:T(8,128)(2,1)} %w_ref.1) | copy-start | bytes 25165828
  30.7 6.3 %copy-start.5 = (s32[9,2]{0,1:T(2,128)S(1)}, s32[9,2]{0,1:T(2,128)}, u32[]{:S(2)}) copy-start(s32[9,2]{0,1:T(2,128)} %param.11) | copy-start | bytes 220
  31.9 18.5 %all-to-all-start = ((bf16[8,2,512]{2,1,0:T(2,128)(2,1)}), bf16[8,2,512]{2,1,0:T(2,128)(2,1)S(1)}, u32[]{:S(2)}, u32[]{:S(2)}) async-start(bf16[8,2,512]{2,1,0:T(2,128)(2,1)} %reshape.17), calls=%async_computation | async-start | bytes 32768 | tf_op jit(solution)/shard_map/all_to_all | solution.py:305
